TPU v7x, 32 devices: a whole 2x2x4 slice. The times are simulated.
32 devices in a mesh: group: 2 (over x), inner: 16 (over z, y, core).
Axes of the slice: x: 2, y: 2, z: 4, core: 2. Of those that a mesh axis runs over, the one named last changes fastest.
Arguments:
- qkv_rows: bfloat16 [4096, 2304], P(('group', 'inner')), parts along dimension 0, may hold values from -8 to 8
- pair_counts: int32 [32, 16], P('group'), parts along dimension 0, may hold values from 0 to 16, as said below
- image_dims: int32 [2, 32], P(None, 'group'), parts along dimension 1, may hold values from 0 to 4, as said below
- block_mask: int32 [32, 7], P(('group', 'inner')), parts along dimension 0, may hold values from 0 to 1, as said below
- out_weight: bfloat16 [768, 1536], replicated, may hold values from -0.21875 to 0.21875
Outputs:
- layer_out: bfloat16 [4096, 1536], P(('group', 'inner')), parts along dimension 0
There are 2 independent parts, one for each index of `group`. A program takes and returns all parts, laid end to end along the dimension named above; an argument that names none is the same for every part. Nothing has to cross between parts.
Inputs may be any that keep to these rules, and one draw needn't show every extreme that they name: `pair_counts`: every row and every column sums to 128, and every row and every column holds an entry equal to 16. `image_dims`: widths are 1, 2 or 4; each image covers at most 4 tiles and some image is 4 tiles high and 1 wide; the tiles of all images sum to 16; images of height 0 stand only after all others. `block_mask`: column 4 - 1 (a tile with itself) is always 1.
All inputs are finite; a program needn't handle non-finite values.
Results may differ from a plain program's by a relative error of at most 0.0093.
Values may be sent and summed in bfloat16 or wider, within the bound.
A program may use at most 64 MiB of HBM per device.

v0:
```python
import math
import jax
import jax.numpy as jnp
from jax import lax
from jax.sharding import PartitionSpec as P

H = 6
HD = 128
TR = 8
TC = 16
SPAN = 4
MAXT = 4
WIN = 7


def from_behind(value, axis, steps):
    count = lax.axis_size(axis)
    pairs = [(source, (source + steps) % count) for source in range(count)]
    return lax.ppermute(value, axis, pairs)


def block_places(blocks, image_dims):
    heights = image_dims[0]
    widths = image_dims[1]
    tile_count = heights * widths
    starts = jnp.cumsum(tile_count) - tile_count
    inside = (starts[None, :] <= blocks[:, None]).astype(jnp.int32)
    image_id = jnp.sum(inside, axis=1) - 1
    picked = jnp.arange(starts.shape[0], dtype=jnp.int32)[None, :] == image_id[:, None]
    first_block = jnp.sum(jnp.where(picked, starts[None, :], 0), axis=1)
    across = jnp.maximum(jnp.sum(jnp.where(picked, widths[None, :], 0), axis=1), 1)
    local_tile = blocks - first_block
    return (image_id, local_tile // across, local_tile % across)


def rotate(rows_in, row_pos, col_pos):
    count = rows_in.shape[0]
    quarter = HD // 4
    frequency = 10000.0 ** (-jnp.arange(quarter, dtype=jnp.float32) / quarter)
    angles = jnp.stack(
        [
            row_pos.astype(jnp.float32)[:, None] * frequency[None, :],
            col_pos.astype(jnp.float32)[:, None] * frequency[None, :],
        ],
        axis=1,
    )
    cosine = jnp.cos(angles)[:, None, :, :]
    sine_part = jnp.sin(angles)[:, None, :, :]
    split_rows = rows_in.astype(jnp.float32).reshape(count, H, 2, 2, quarter)
    leading = split_rows[:, :, :, 0, :]
    trailing = split_rows[:, :, :, 1, :]
    turned = jnp.stack(
        [leading * cosine - trailing * sine_part, trailing * cosine + leading * sine_part], axis=3
    )
    return turned.reshape(count, H * HD).astype(jnp.bfloat16)


def shards(qkv_rows, pair_counts, image_dims, block_mask, out_weight):
    devices = lax.axis_size("inner")
    self_index = lax.axis_index("inner")
    tok_rows = qkv_rows.shape[0]
    full_width = qkv_rows.shape[1]
    inner_width = full_width // 3
    slot_count = 2 * tok_rows // devices
    block_rows = TR * TC
    per_device = tok_rows // block_rows
    reach_count = (SPAN * tok_rows - block_rows + tok_rows - 1) // tok_rows
    score_scale = 1.0 / math.sqrt(HD)
    sent_counts = lax.dynamic_index_in_dim(pair_counts, self_index, 0, keepdims=False)
    taken_counts = lax.dynamic_index_in_dim(pair_counts, self_index, 1, keepdims=False)
    sent_end = jnp.cumsum(sent_counts)
    sent_start = sent_end - sent_counts
    taken_end = jnp.cumsum(taken_counts)
    taken_start = taken_end - taken_counts
    slot_ids = jnp.arange(slot_count, dtype=jnp.int32)
    row_ids = jnp.arange(tok_rows, dtype=jnp.int32)
    peer_ids = jnp.arange(devices, dtype=jnp.int32)
    outgoing = jnp.minimum(sent_start[:, None] + slot_ids[None, :], tok_rows - 1).reshape(-1)
    parcels = jnp.take(qkv_rows, outgoing, axis=0).reshape(devices, slot_count, full_width)
    arrived = lax.all_to_all(parcels, "inner", split_axis=0, concat_axis=0, tiled=True)
    source = jnp.sum((taken_end[None, :] <= row_ids[:, None]).astype(jnp.int32), axis=1)
    is_source = source[:, None] == peer_ids[None, :]
    offset_in = row_ids - jnp.sum(jnp.where(is_source, taken_start[None, :], 0), axis=1)
    incoming = source * slot_count + offset_in
    owned_rows = jnp.take(arrived.reshape(devices * slot_count, full_width), incoming, axis=0)
    query_blocks = self_index * per_device + jnp.arange(per_device, dtype=jnp.int32)
    query_image, tile_row, tile_col = block_places(query_blocks, image_dims)
    within = jnp.arange(block_rows, dtype=jnp.int32)
    row_pos = (tile_row[:, None] * TR + within[None, :] // TC).reshape(-1)
    col_pos = (tile_col[:, None] * TC + within[None, :] % TC).reshape(-1)
    queries = rotate(owned_rows[:, :inner_width], row_pos, col_pos).reshape(tok_rows, H, HD)
    keys = rotate(owned_rows[:, inner_width : 2 * inner_width], row_pos, col_pos)
    key_value = jnp.stack([keys, owned_rows[:, 2 * inner_width :]])

    def absorb(softmax_state, key_piece, allowed):
        row_max, row_sum, summed = softmax_state
        visible = jnp.repeat(jnp.repeat(allowed, block_rows, axis=0), block_rows, axis=1)[
            :, None, :
        ]
        far_keys = key_piece[0].reshape(tok_rows, H, HD)
        far_values = key_piece[1].reshape(tok_rows, H, HD)
        scores = (
            jnp.einsum("qhd,khd->qhk", queries, far_keys, preferred_element_type=jnp.float32)
            * score_scale
        )
        scores = jnp.where(visible, scores, -1e30)
        new_max = jnp.maximum(row_max, jnp.max(scores, axis=2))
        weights = jnp.where(visible, jnp.exp(scores - new_max[:, :, None]), 0.0)
        rescale = jnp.exp(row_max - new_max)
        row_sum = row_sum * rescale + jnp.sum(weights, axis=2)
        summed = summed * rescale[:, :, None] + jnp.einsum(
            "qhk,khd->qhd",
            weights.astype(jnp.bfloat16),
            far_values,
            preferred_element_type=jnp.float32,
        )
        return (new_max, row_sum, summed)

    def visit(softmax_state, key_piece, source_dev):
        key_blocks = source_dev * per_device + jnp.arange(per_device, dtype=jnp.int32)
        key_image = block_places(key_blocks, image_dims)[0]
        offset = key_blocks[None, :] - query_blocks[:, None] + (MAXT - 1)
        mask_bits = jnp.take_along_axis(block_mask, jnp.clip(offset, 0, WIN - 1), axis=1)
        allowed = (
            (offset >= 0)
            & (offset < WIN)
            & (mask_bits == 1)
            & (query_image[:, None] == key_image[None, :])
            & (source_dev >= 0)
            & (source_dev < devices)
        )
        return absorb(softmax_state, key_piece, allowed)

    initial = (
        jnp.full((tok_rows, H), -1e30, jnp.float32),
        jnp.zeros((tok_rows, H), jnp.float32),
        jnp.zeros((tok_rows, H, HD), jnp.float32),
    )
    farthest = from_behind(key_value, "inner", -reach_count)
    softmax_state = visit(initial, farthest, self_index + reach_count)

    def one_way(hop_index, carry):
        key_piece, running = carry
        key_piece = from_behind(key_piece, "inner", 1)
        return (key_piece, visit(running, key_piece, self_index + reach_count - hop_index - 1))

    softmax_state = lax.fori_loop(0, 2 * reach_count, one_way, (farthest, softmax_state))[1]
    row_max, row_sum, summed = softmax_state
    attended = (summed / row_sum[:, :, None]).reshape(tok_rows, H * HD).astype(jnp.bfloat16)
    projected = jnp.dot(attended, out_weight, preferred_element_type=jnp.float32).astype(
        jnp.bfloat16
    )
    out_width = projected.shape[1]
    back_slots = jnp.minimum(taken_start[:, None] + slot_ids[None, :], tok_rows - 1).reshape(-1)
    returning = jnp.take(projected, back_slots, axis=0).reshape(devices, slot_count, out_width)
    returned = lax.all_to_all(returning, "inner", split_axis=0, concat_axis=0, tiled=True)
    target = jnp.sum((sent_end[None, :] <= row_ids[:, None]).astype(jnp.int32), axis=1)
    is_target = target[:, None] == peer_ids[None, :]
    offset_back = row_ids - jnp.sum(jnp.where(is_target, sent_start[None, :], 0), axis=1)
    return jnp.take(
        returned.reshape(devices * slot_count, out_width), target * slot_count + offset_back, axis=0
    )


def solution(mesh):
    in_specs = (
        P(("group", "inner"), None),
        P("group", None),
        P(None, "group"),
        P(("group", "inner"), None),
        P(),
    )
    out_specs = P(("group", "inner"), None)
    return jax.shard_map(shards, mesh=mesh, in_specs=in_specs, out_specs=out_specs, check_vma=False)
```

profile of v0, /device:TPU:11, one launch (start us, length us, event | category | flops | bytes accessed | tf_op | source)
XLA Modules:
  0.0 164.5 jit_solution(5951095822573143242)
XLA Ops:
  0.0 0.8 fusion.36
  2.5 3.7 %gather_fusion = bf16[256,2304]{1,0:T(8,128)(2,1)S(1)} fusion(bf16[128,2304]{1,0:T(8,128)(2,1)} %param.7, s32[1024]{0:T(1024)S(1)} %pad_clamp_fusion.3), kind=kCustom, calls=%fused_computation | custom fusion | bytes 2360320 | tf_op jit(solution)/shard_map/jit(_take)/gather | solution.py:79
  6.3 1.2 broadcast_select_fusion
  7.4 6.7 %all-to-all-start = ((bf16[16,16,2304]{2,1,0:T(8,128)(2,1)}), bf16[16,16,2304]{2,1,0:T(8,128)(2,1)S(1)}, u32[]{:S(2)}, u32[]{:S(2)}) async-start(bf16[16,16,2304]{2,1,0:T(8,128)(2,1)} %broadcast_select_fusion), calls=%async_computation | async-start | bytes 2359296 | tf_op jit(solution)/shard_map/all_to_all | solution.py:80
  14.9 1.4 fusion.28
  20.3 0.7 reduce-window.13
  21.0 0.8 subtract_reduce_fusion
  23.7 0.7 convert_reduce_fusion
  24.6 0.8 fusion.21
  26.6 15.2 %all-to-all-done = bf16[16,16,2304]{2,1,0:T(8,128)(2,1)S(1)} async-done(((bf16[16,16,2304]{2,1,0:T(8,128)(2,1)}), bf16[16,16,2304]{2,1,0:T(8,128)(2,1)S(1)}, u32[]{:S(2)}, u32[]{:S(2)}) %all-to-all-start) | async-done | bytes 1179680 | tf_op jit(solution)/shard_map/all_to_all | solution.py:80
  41.7 1.8 %gather_fusion.1 = bf16[128,2304]{1,0:T(8,128)(2,1)} fusion(bf16[256,2304]{1,0:T(8,128)(2,1)S(1)} %bitcast.110, s32[1024]{0:T(1024)S(1)} %pad_clamp_fusion.2), kind=kCustom, calls=%fused_computation.1 | custom fusion | bytes 1180160 | tf_op jit(solution)/shard_map/jit(_take)/gather | solution.py:85
  43.5 1.2 broadcast_select_fusion.2
  44.7 0.7 slice_convert_fusion
  45.8 1.6 subtract_convert_fusion
  47.6 0.8 pad_maximum_fusion
  51.8 7.9 %collective-permute-done.1 = bf16[2,128,768]{2,1,0:T(8,128)(2,1)S(1)} collective-permute-done((bf16[2,128,768]{2,1,0:T(8,128)(2,1)}, bf16[2,128,768]{2,1,0:T(8,128)(2,1)S(1)}, u32[]{:S(2)}, u32[]{:S(2)}) %collective-permute-start.1) | collective-permute-done | bytes 393248 | tf_op jit(solution)/shard_map/ppermute | solution.py:19
  59.7 0.7 fusion.41
  60.4 0.8 copy.38
  61.2 1.2 fusion.42
  63.1 1.1 copy.42
  64.2 1.6 fusion.11
  65.8 1.2 copy.45
  67.0 0.9 copy.44
  68.0 53.5 %while.24 = (s32[]{:T(128)}, bf16[2,128,768]{1,2,0:T(8,128)(2,1)}, f32[128,6]{0,1:T(8,128)S(1)}, f32[128,6]{0,1:T(8,128)S(1)}, f32[128,6,128]{2,0,1:T(8,128)S(1)...) while((s32[]{:T(128)}, bf16[2,128,768]{1,2,0:T(8,128)(2,1)}, ...), condition=%wide.region_17.18_spmd, body=%wide.region_13.17_spmd.sunk | while | flops 51414596 | bytes 5751247 | solution.py:147
  68.0 2.2 %collective-permute-start = (bf16[2,128,768]{1,2,0:T(8,128)(2,1)}, bf16[2,128,768]{1,2,0:T(8,128)(2,1)S(1)}, u32[]{:S(2)}, u32[]{:S(2)}) collective-permute-start(bf16[2,128,768]{1,2,0:T(8,128)(2,1)} %get-tuple-element.481), channel_id=1, source_target_pairs={{0,1},{1,2},{2,3},{3,4},{4,5},{5,6},{6,7},{7,8},{8,9},{9,10},{10,1... | collective-permute-start | bytes 1179656 | tf_op jit(solution)/shard_map/while/body/eval_jaxpr/ppermute | solution.py:19
  72.7 2.5 %collective-permute-done = bf16[2,128,768]{1,2,0:T(8,128)(2,1)S(1)} collective-permute-done((bf16[2,128,768]{1,2,0:T(8,128)(2,1)}, bf16[2,128,768]{1,2,0:T(8,128)(2,1)S(1)}, u32[]{:S(2)}, u32[]{:S(2)}) %collective-permute-start) | collective-permute-done | bytes 393248 | tf_op jit(solution)/shard_map/while/body/eval_jaxpr/ppermute | solution.py:19
  76.0 0.7 copy.65
  76.7 2.4 %collective-permute-start = (bf16[2,128,768]{1,2,0:T(8,128)(2,1)}, bf16[2,128,768]{1,2,0:T(8,128)(2,1)S(1)}, u32[]{:S(2)}, u32[]{:S(2)}) collective-permute-start(bf16[2,128,768]{1,2,0:T(8,128)(2,1)} %get-tuple-element.481), channel_id=1, source_target_pairs={{0,1},{1,2},{2,3},{3,4},{4,5},{5,6},{6,7},{7,8},{8,9},{9,10},{10,1... | collective-permute-start | bytes 1179656 | tf_op jit(solution)/shard_map/while/body/eval_jaxpr/ppermute | solution.py:19
  81.6 2.5 %collective-permute-done = bf16[2,128,768]{1,2,0:T(8,128)(2,1)S(1)} collective-permute-done((bf16[2,128,768]{1,2,0:T(8,128)(2,1)}, bf16[2,128,768]{1,2,0:T(8,128)(2,1)S(1)}, u32[]{:S(2)}, u32[]{:S(2)}) %collective-permute-start) | collective-permute-done | bytes 393248 | tf_op jit(solution)/shard_map/while/body/eval_jaxpr/ppermute | solution.py:19
  84.9 0.7 copy.65
  85.7 2.4 %collective-permute-start = (bf16[2,128,768]{1,2,0:T(8,128)(2,1)}, bf16[2,128,768]{1,2,0:T(8,128)(2,1)S(1)}, u32[]{:S(2)}, u32[]{:S(2)}) collective-permute-start(bf16[2,128,768]{1,2,0:T(8,128)(2,1)} %get-tuple-element.481), channel_id=1, source_target_pairs={{0,1},{1,2},{2,3},{3,4},{4,5},{5,6},{6,7},{7,8},{8,9},{9,10},{10,1... | collective-permute-start | bytes 1179656 | tf_op jit(solution)/shard_map/while/body/eval_jaxpr/ppermute | solution.py:19
  90.6 2.5 %collective-permute-done = bf16[2,128,768]{1,2,0:T(8,128)(2,1)S(1)} collective-permute-done((bf16[2,128,768]{1,2,0:T(8,128)(2,1)}, bf16[2,128,768]{1,2,0:T(8,128)(2,1)S(1)}, u32[]{:S(2)}, u32[]{:S(2)}) %collective-permute-start) | collective-permute-done | bytes 393248 | tf_op jit(solution)/shard_map/while/body/eval_jaxpr/ppermute | solution.py:19
  93.9 0.7 copy.65
  94.6 2.4 %collective-permute-start = (bf16[2,128,768]{1,2,0:T(8,128)(2,1)}, bf16[2,128,768]{1,2,0:T(8,128)(2,1)S(1)}, u32[]{:S(2)}, u32[]{:S(2)}) collective-permute-start(bf16[2,128,768]{1,2,0:T(8,128)(2,1)} %get-tuple-element.481), channel_id=1, source_target_pairs={{0,1},{1,2},{2,3},{3,4},{4,5},{5,6},{6,7},{7,8},{8,9},{9,10},{10,1... | collective-permute-start | bytes 1179656 | tf_op jit(solution)/shard_map/while/body/eval_jaxpr/ppermute | solution.py:19
  99.5 2.5 %collective-permute-done = bf16[2,128,768]{1,2,0:T(8,128)(2,1)S(1)} collective-permute-done((bf16[2,128,768]{1,2,0:T(8,128)(2,1)}, bf16[2,128,768]{1,2,0:T(8,128)(2,1)S(1)}, u32[]{:S(2)}, u32[]{:S(2)}) %collective-permute-start) | collective-permute-done | bytes 393248 | tf_op jit(solution)/shard_map/while/body/eval_jaxpr/ppermute | solution.py:19
  102.8 0.7 copy.65
  103.6 2.4 %collective-permute-start = (bf16[2,128,768]{1,2,0:T(8,128)(2,1)}, bf16[2,128,768]{1,2,0:T(8,128)(2,1)S(1)}, u32[]{:S(2)}, u32[]{:S(2)}) collective-permute-start(bf16[2,128,768]{1,2,0:T(8,128)(2,1)} %get-tuple-element.481), channel_id=1, source_target_pairs={{0,1},{1,2},{2,3},{3,4},{4,5},{5,6},{6,7},{7,8},{8,9},{9,10},{10,1... | collective-permute-start | bytes 1179656 | tf_op jit(solution)/shard_map/while/body/eval_jaxpr/ppermute | solution.py:19
  108.5 2.5 %collective-permute-done = bf16[2,128,768]{1,2,0:T(8,128)(2,1)S(1)} collective-permute-done((bf16[2,128,768]{1,2,0:T(8,128)(2,1)}, bf16[2,128,768]{1,2,0:T(8,128)(2,1)S(1)}, u32[]{:S(2)}, u32[]{:S(2)}) %collective-permute-start) | collective-permute-done | bytes 393248 | tf_op jit(solution)/shard_map/while/body/eval_jaxpr/ppermute | solution.py:19
  111.8 0.7 copy.65
  112.5 2.4 %collective-permute-start = (bf16[2,128,768]{1,2,0:T(8,128)(2,1)}, bf16[2,128,768]{1,2,0:T(8,128)(2,1)S(1)}, u32[]{:S(2)}, u32[]{:S(2)}) collective-permute-start(bf16[2,128,768]{1,2,0:T(8,128)(2,1)} %get-tuple-element.481), channel_id=1, source_target_pairs={{0,1},{1,2},{2,3},{3,4},{4,5},{5,6},{6,7},{7,8},{8,9},{9,10},{10,1... | collective-permute-start | bytes 1179656 | tf_op jit(solution)/shard_map/while/body/eval_jaxpr/ppermute | solution.py:19
  117.4 2.5 %collective-permute-done = bf16[2,128,768]{1,2,0:T(8,128)(2,1)S(1)} collective-permute-done((bf16[2,128,768]{1,2,0:T(8,128)(2,1)}, bf16[2,128,768]{1,2,0:T(8,128)(2,1)S(1)}, u32[]{:S(2)}, u32[]{:S(2)}) %collective-permute-start) | collective-permute-done | bytes 393248 | tf_op jit(solution)/shard_map/while/body/eval_jaxpr/ppermute | solution.py:19
  120.7 0.7 copy.65
  122.2 1.4 gather_fusion.2
  123.6 1.0 broadcast_select_fusion.1
  124.6 18.5 %all-to-all-start.1 = ((bf16[16,16,1536]{2,1,0:T(8,128)(2,1)}), bf16[16,16,1536]{2,1,0:T(8,128)(2,1)S(1)}, u32[]{:S(2)}, u32[]{:S(2)}) async-start(bf16[16,16,1536]{2,1,0:T(8,128)(2,1)} %broadcast_select_fusion.1), calls=%async_computation.1 | async-start | bytes 1572864 | tf_op jit(solution)/shard_map/all_to_all | solution.py:156
  143.4 19.4 %all-to-all-done.1 = bf16[16,16,1536]{2,1,0:T(8,128)(2,1)S(1)} async-done(((bf16[16,16,1536]{2,1,0:T(8,128)(2,1)}), bf16[16,16,1536]{2,1,0:T(8,128)(2,1)S(1)}, u32[]{:S(2)}, u32[]{:S(2)}) %all-to-all-start.1) | async-done | bytes 786464 | tf_op jit(solution)/shard_map/all_to_all | solution.py:156
  162.8 0.9 gather_fusion.3
  163.7 0.9 broadcast_select_fusion.3
  (131 shorter events, 23.9 us)
Async XLA Ops:
  0.0 121.7 %copy-start = (bf16[768,1536]{1,0:T(8,128)(2,1)S(1)}, bf16[768,1536]{1,0:T(8,128)(2,1)}, u32[]{:S(2)}) copy-start(bf16[768,1536]{1,0:T(8,128)(2,1)} %param.11) | copy-start | bytes 7077892
  1.1 0.5 copy-start.10
  7.4 6.7 %copy-start.14 = (s32[2,16]{1,0:T(2,128)S(1)}, s32[2,16]{1,0:T(2,128)}, u32[]{:S(2)}) copy-start(s32[2,16]{1,0:T(2,128)} %param.9) | copy-start | bytes 388
  7.4 12.1 %copy-start.4 = (s32[16,16]{1,0:T(8,128)S(1)}, s32[16,16]{1,0:T(8,128)}, u32[]{:S(2)}) copy-start(s32[16,16]{1,0:T(8,128)} %param.8) | copy-start | bytes 3076
  7.4 34.3 %all-to-all-start = ((bf16[16,16,2304]{2,1,0:T(8,128)(2,1)}), bf16[16,16,2304]{2,1,0:T(8,128)(2,1)S(1)}, u32[]{:S(2)}, u32[]{:S(2)}) async-start(bf16[16,16,2304]{2,1,0:T(8,128)(2,1)} %broadcast_select_fusion), calls=%async_computation | async-start | bytes 2359296 | tf_op jit(solution)/shard_map/all_to_all | solution.py:80
  16.3 3.3 %copy-start.12 = (s32[1,16]{1,0:T(1,128)}, s32[1,16]{1,0:T(1,128)S(1)}, u32[]{:S(2)}) copy-start(s32[1,16]{1,0:T(1,128)S(1)} %get-tuple-element.469) | copy-start | bytes 196
  21.7 0.5 copy-start.8
  45.8 1.8 %copy-start.1 = (bf16[1,128,768]{2,1,0:T(8,128)(2,1)S(1)}, bf16[1,128,768]{2,1,0:T(8,128)(2,1)}, u32[]{:S(2)}) copy-start(bf16[1,128,768]{2,1,0:T(8,128)(2,1)} %get-tuple-element.362) | copy-start | bytes 589828
  45.8 3.2 %copy-start.5 = (s32[1,7]{1,0:T(1,128)S(1)}, s32[1,7]{1,0:T(1,128)}, u32[]{:S(2)}) copy-start(s32[1,7]{1,0:T(1,128)} %param.10) | copy-start | bytes 88
  45.8 5.1 %copy-start.9 = (s32[16]{0:T(128)S(1)}, s32[16]{0:T(128)}, u32[]{:S(2)}) copy-start(s32[16]{0:T(128)} %copy-done.8) | copy-start | bytes 196
  47.4 4.2 %copy-start.2 = (bf16[128,6,2,1,32]{0,4,3,2,1:T(8,128)(2,1)S(1)}, bf16[128,6,2,1,32]{0,4,3,2,1:T(8,128)(2,1)}, u32[]{:S(2)}) copy-start(bf16[128,6,2,1,32]{0,4,3,2,1:T(8,128)(2,1)} %get-tuple-element.364) | copy-start | bytes 294916
  47.4 4.2 %copy-start.3 = (bf16[128,6,2,1,32]{0,4,3,2,1:T(8,128)(2,1)S(1)}, bf16[128,6,2,1,32]{0,4,3,2,1:T(8,128)(2,1)}, u32[]{:S(2)}) copy-start(bf16[128,6,2,1,32]{0,4,3,2,1:T(8,128)(2,1)} %get-tuple-element.365) | copy-start | bytes 294916
  48.4 11.3 %collective-permute-start.1 = (bf16[2,128,768]{2,1,0:T(8,128)(2,1)}, bf16[2,128,768]{2,1,0:T(8,128)(2,1)S(1)}, u32[]{:S(2)}, u32[]{:S(2)}) collective-permute-start(bf16[2,128,768]{2,1,0:T(8,128)(2,1)} %pad_maximum_fusion), channel_id=1, source_target_pairs={{0,13},{1,14},{2,15},{3,0},{4,1},{5,2},{6,3},{7,4},{8,5},{9,6},{10... | collective-permute-start | bytes 1179656 | tf_op jit(solution)/shard_map/ppermute | solution.py:19
  65.8 2.1 %copy-start.6 = (s32[1,7]{1,0:T(1,128)S(1)}, s32[1,7]{1,0:T(1,128)}, u32[]{:S(2)}) copy-start(s32[1,7]{1,0:T(1,128)} %param.10) | copy-start | bytes 88
  65.8 2.1 %copy-start.13 = (s32[1,16]{1,0:T(1,128)S(1)}, s32[1,16]{1,0:T(1,128)}, u32[]{:S(2)}) copy-start(s32[1,16]{1,0:T(1,128)} %copy-done.12) | copy-start | bytes 196
  68.0 7.2 %collective-permute-start = (bf16[2,128,768]{1,2,0:T(8,128)(2,1)}, bf16[2,128,768]{1,2,0:T(8,128)(2,1)S(1)}, u32[]{:S(2)}, u32[]{:S(2)}) collective-permute-start(bf16[2,128,768]{1,2,0:T(8,128)(2,1)} %get-tuple-element.481), channel_id=1, source_target_pairs={{0,1},{1,2},{2,3},{3,4},{4,5},{5,6},{6,7},{7,8},{8,9},{9,10},{10,1... | collective-permute-start | bytes 1179656 | tf_op jit(solution)/shard_map/while/body/eval_jaxpr/ppermute | solution.py:19
  76.7 7.4 %collective-permute-start = (bf16[2,128,768]{1,2,0:T(8,128)(2,1)}, bf16[2,128,768]{1,2,0:T(8,128)(2,1)S(1)}, u32[]{:S(2)}, u32[]{:S(2)}) collective-permute-start(bf16[2,128,768]{1,2,0:T(8,128)(2,1)} %get-tuple-element.481), channel_id=1, source_target_pairs={{0,1},{1,2},{2,3},{3,4},{4,5},{5,6},{6,7},{7,8},{8,9},{9,10},{10,1... | collective-permute-start | bytes 1179656 | tf_op jit(solution)/shard_map/while/body/eval_jaxpr/ppermute | solution.py:19
  85.7 7.4 %collective-permute-start = (bf16[2,128,768]{1,2,0:T(8,128)(2,1)}, bf16[2,128,768]{1,2,0:T(8,128)(2,1)S(1)}, u32[]{:S(2)}, u32[]{:S(2)}) collective-permute-start(bf16[2,128,768]{1,2,0:T(8,128)(2,1)} %get-tuple-element.481), channel_id=1, source_target_pairs={{0,1},{1,2},{2,3},{3,4},{4,5},{5,6},{6,7},{7,8},{8,9},{9,10},{10,1... | collective-permute-start | bytes 1179656 | tf_op jit(solution)/shard_map/while/body/eval_jaxpr/ppermute | solution.py:19
  94.6 7.4 %collective-permute-start = (bf16[2,128,768]{1,2,0:T(8,128)(2,1)}, bf16[2,128,768]{1,2,0:T(8,128)(2,1)S(1)}, u32[]{:S(2)}, u32[]{:S(2)}) collective-permute-start(bf16[2,128,768]{1,2,0:T(8,128)(2,1)} %get-tuple-element.481), channel_id=1, source_target_pairs={{0,1},{1,2},{2,3},{3,4},{4,5},{5,6},{6,7},{7,8},{8,9},{9,10},{10,1... | collective-permute-start | bytes 1179656 | tf_op jit(solution)/shard_map/while/body/eval_jaxpr/ppermute | solution.py:19
  103.6 7.4 %collective-permute-start = (bf16[2,128,768]{1,2,0:T(8,128)(2,1)}, bf16[2,128,768]{1,2,0:T(8,128)(2,1)S(1)}, u32[]{:S(2)}, u32[]{:S(2)}) collective-permute-start(bf16[2,128,768]{1,2,0:T(8,128)(2,1)} %get-tuple-element.481), channel_id=1, source_target_pairs={{0,1},{1,2},{2,3},{3,4},{4,5},{5,6},{6,7},{7,8},{8,9},{9,10},{10,1... | collective-permute-start | bytes 1179656 | tf_op jit(solution)/shard_map/while/body/eval_jaxpr/ppermute | solution.py:19
  112.5 7.4 %collective-permute-start = (bf16[2,128,768]{1,2,0:T(8,128)(2,1)}, bf16[2,128,768]{1,2,0:T(8,128)(2,1)S(1)}, u32[]{:S(2)}, u32[]{:S(2)}) collective-permute-start(bf16[2,128,768]{1,2,0:T(8,128)(2,1)} %get-tuple-element.481), channel_id=1, source_target_pairs={{0,1},{1,2},{2,3},{3,4},{4,5},{5,6},{6,7},{7,8},{8,9},{9,10},{10,1... | collective-permute-start | bytes 1179656 | tf_op jit(solution)/shard_map/while/body/eval_jaxpr/ppermute | solution.py:19
  122.2 1.4 copy-start.7
  124.6 18.5 %copy-start.11 = (s32[16]{0:T(128)S(1)}, s32[16]{0:T(128)}, u32[]{:S(2)}) copy-start(s32[16]{0:T(128)} %copy-done.10) | copy-start | bytes 196
  124.6 38.1 %all-to-all-start.1 = ((bf16[16,16,1536]{2,1,0:T(8,128)(2,1)}), bf16[16,16,1536]{2,1,0:T(8,128)(2,1)S(1)}, u32[]{:S(2)}, u32[]{:S(2)}) async-start(bf16[16,16,1536]{2,1,0:T(8,128)(2,1)} %broadcast_select_fusion.1), calls=%async_computation.1 | async-start | bytes 1572864 | tf_op jit(solution)/shard_map/all_to_all | solution.py:156
where the time goes:
time: 165 us
  waiting for transfers between devices  57.5 us (35%)
  starting transfers between devices  39.3 us (24%)
  other arithmetic  27.2 us (16%)
  local copies, waits for them, and re-layouts  21.9 us (13%)
  loops' own time  7.9 us (5%)
  matrix products  7.06 us (4%)
  between operations  3.53 us (2%)
    ppermute x7, waiting for transfers between devices, from_behind(): return lax.ppermute(value, axis, pairs)  23 us
    all_to_all x1, waiting for transfers between devices, shards(): lax.all_to_all(returning, 'inner', split_axis=0, concat_axis=0, tiled=True)  19.4 us
    all_to_all x1, starting transfers between devices, shards(): lax.all_to_all(returning, 'inner', split_axis=0, concat_axis=0, tiled=True)  18.5 us
    all_to_all x1, waiting for transfers between devices, shards(): lax.all_to_all(parcels, 'inner', split_axis=0, concat_axis=0, tiled=True)  15.2 us
    ppermute x7, starting transfers between devices, from_behind(): return lax.ppermute(value, axis, pairs)  14.1 us
    another operation x1, loops' own time, shards(): lax.fori_loop(0, 2 * reach_count, one_way, (farthest, softmax_state))[1]  7.9 us
    all_to_all x1, starting transfers between devices, shards(): lax.all_to_all(parcels, 'inner', split_axis=0, concat_axis=0, tiled=True)  6.74 us
    reduce_sum x8, other arithmetic, block_places(): image_id = jnp.sum(inside, axis=1) - 1  5.9 us
  transfers between devices with their start and end apart: 9, of which 9 were waited for; matrix products, arithmetic and copies ran while one was open for 12% of the time, Pallas kernels for 0%

commit v1 on v0

--- a/solution.py
+++ b/solution.py
@@ -11,6 +11,27 @@
 SPAN = 4
 MAXT = 4
 WIN = 7
+
+
+def _do_panels(xs):
+    lane_axis = "inner"
+    high, v_next = (lax.axis_size(lane_axis), lax.axis_index(lane_axis))
+    o_now = xs.shape[0] // high
+    odd = list(xs.shape)
+    odd[0] = o_now
+    q_next = odd[0]
+    odd[0] = q_next * high
+    piece_out = jnp.zeros(odd, xs.dtype)
+    for dev in [*range(high)]:
+        x_next = lax.dynamic_slice_in_dim(xs, (v_next ^ dev) * o_now, o_now, axis=0)
+        if dev:
+            x_next = lax.ppermute(
+                x_next, axis_name=lane_axis, perm=tuple(((idx, idx ^ dev) for idx in range(high)))
+            )
+        piece_out = lax.dynamic_update_slice_in_dim(
+            piece_out, x_next, (v_next ^ dev) * q_next, axis=0
+        )
+    return piece_out
 
 
 def from_behind(value, axis, steps):
@@ -153,7 +174,7 @@
     out_width = projected.shape[1]
     back_slots = jnp.minimum(taken_start[:, None] + slot_ids[None, :], tok_rows - 1).reshape(-1)
     returning = jnp.take(projected, back_slots, axis=0).reshape(devices, slot_count, out_width)
-    returned = lax.all_to_all(returning, "inner", split_axis=0, concat_axis=0, tiled=True)
+    returned = _do_panels(returning)
     target = jnp.sum((sent_end[None, :] <= row_ids[:, None]).astype(jnp.int32), axis=1)
     is_target = target[:, None] == peer_ids[None, :]
     offset_back = row_ids - jnp.sum(jnp.where(is_target, sent_start[None, :], 0), axis=1)

time: 165 us -> 170 us (1.030); the launches traced: 165 us -> 168 us
  starting transfers between devices: 39.3 us -> 52 us
  waiting for transfers between devices: 57.5 us -> 50.4 us
    ppermute x0 -> x15, starting transfers between devices: none -> 31.1 us  [_do_panels(): lax.ppermute(x_next, axis_name=lane_axis, perm=tuple(((idx, idx ^ dev) fo...]
    all_to_all x1 -> x0, waiting for transfers between devices: 19.4 us -> none  [shards(): lax.all_to_all(returning, 'inner', split_axis=0, concat_axis=0, tiled=True)]
    all_to_all x1 -> x0, starting transfers between devices: 18.5 us -> none  [shards(): lax.all_to_all(returning, 'inner', split_axis=0, concat_axis=0, tiled=True)]
    ppermute x0 -> x15, waiting for transfers between devices: none -> 8.75 us  [_do_panels(): lax.ppermute(x_next, axis_name=lane_axis, perm=tuple(((idx, idx ^ dev) fo...]
    all_to_all x1, waiting for transfers between devices: 15.2 us -> 19 us  [shards(): lax.all_to_all(parcels, 'inner', split_axis=0, concat_axis=0, tiled=True)]
  transfers between devices with their start and end apart: 9 -> 23, of which waited for: 9 -> 11; matrix products, arithmetic and copies ran while one was open for 12% -> 10% of each run, Pallas kernels for 0% -> 0%
where the time goes in v1:
time: 170 us; the launch traced here: 168 us
  starting transfers between devices  52 us (31%)
  waiting for transfers between devices  50.4 us (30%)
  other arithmetic  26.6 us (16%)
  local copies, waits for them, and re-layouts  20.7 us (12%)
  loops' own time  7.96 us (5%)
  matrix products  6.38 us (4%)
  between operations  3.57 us (2%)
    ppermute x15, starting transfers between devices, _do_panels(): lax.ppermute(x_next, axis_name=lane_axis, perm=tuple(((idx, idx ^ dev) fo...  31.1 us
    ppermute x7, waiting for transfers between devices, from_behind(): return lax.ppermute(value, axis, pairs)  22.7 us
    all_to_all x1, waiting for transfers between devices, shards(): lax.all_to_all(parcels, 'inner', split_axis=0, concat_axis=0, tiled=True)  19 us
    ppermute x7, starting transfers between devices, from_behind(): return lax.ppermute(value, axis, pairs)  14.1 us
    ppermute x15, waiting for transfers between devices, _do_panels(): lax.ppermute(x_next, axis_name=lane_axis, perm=tuple(((idx, idx ^ dev) fo...  8.75 us
    another operation x1, loops' own time, shards(): lax.fori_loop(0, 2 * reach_count, one_way, (farthest, softmax_state))[1]  7.96 us
    all_to_all x1, starting transfers between devices, shards(): lax.all_to_all(parcels, 'inner', split_axis=0, concat_axis=0, tiled=True)  6.74 us
    reduce_sum x8, other arithmetic, block_places(): image_id = jnp.sum(inside, axis=1) - 1  6.01 us
  transfers between devices with their start and end apart: 23, of which 11 were waited for; matrix products, arithmetic and copies ran while one was open for 10% of the time, Pallas kernels for 0%

profile of v1, /device:TPU:11, one launch (start us, length us, event | category | flops | bytes accessed | tf_op | source)
XLA Modules:
  0.0 167.6 jit_solution(5525317768762960952)
XLA Ops:
  0.0 0.8 fusion.36
  0.8 0.8 constant_dynamic-slice_fusion.16
  2.7 1.4 subtract_reduce_fusion
  5.6 3.7 %gather_fusion = bf16[256,2304]{1,0:T(8,128)(2,1)S(1)} fusion(bf16[128,2304]{1,0:T(8,128)(2,1)} %param.7, s32[1024]{0:T(1024)S(1)} %pad_clamp_fusion.3), kind=kCustom, calls=%fused_computation | custom fusion | bytes 2360320 | tf_op jit(solution)/shard_map/jit(_take)/gather | solution.py:100
  9.3 1.2 broadcast_select_fusion
  10.5 6.7 %all-to-all-start = ((bf16[16,16,2304]{2,1,0:T(8,128)(2,1)}), bf16[16,16,2304]{2,1,0:T(8,128)(2,1)S(1)}, u32[]{:S(2)}, u32[]{:S(2)}) async-start(bf16[16,16,2304]{2,1,0:T(8,128)(2,1)} %broadcast_select_fusion), calls=%async_computation | async-start | bytes 2359296 | tf_op jit(solution)/shard_map/all_to_all | solution.py:101
  17.2 0.8 reduce-window_2_clone.1
  18.0 1.3 fusion.28
  25.8 19.0 %all-to-all-done = bf16[16,16,2304]{2,1,0:T(8,128)(2,1)S(1)} async-done(((bf16[16,16,2304]{2,1,0:T(8,128)(2,1)}), bf16[16,16,2304]{2,1,0:T(8,128)(2,1)S(1)}, u32[]{:S(2)}, u32[]{:S(2)}) %all-to-all-start) | async-done | bytes 1179680 | tf_op jit(solution)/shard_map/all_to_all | solution.py:101
  44.8 1.8 %gather_fusion.1 = bf16[128,2304]{1,0:T(8,128)(2,1)} fusion(bf16[256,2304]{1,0:T(8,128)(2,1)S(1)} %bitcast.110, s32[1024]{0:T(1024)S(1)} %pad_clamp_fusion.2), kind=kCustom, calls=%fused_computation.1 | custom fusion | bytes 1180160 | tf_op jit(solution)/shard_map/jit(_take)/gather | solution.py:106
  46.5 1.2 broadcast_select_fusion.2
  48.8 1.6 subtract_convert_fusion
  50.6 0.8 pad_maximum_fusion
  54.7 8.1 %collective-permute-done.1 = bf16[2,128,768]{2,1,0:T(8,128)(2,1)S(1)} collective-permute-done((bf16[2,128,768]{2,1,0:T(8,128)(2,1)}, bf16[2,128,768]{2,1,0:T(8,128)(2,1)S(1)}, u32[]{:S(2)}, u32[]{:S(2)}) %collective-permute-start.1) | collective-permute-done | bytes 393248 | tf_op jit(solution)/shard_map/ppermute | solution.py:40
  63.4 0.8 copy.38
  64.2 1.2 fusion.42
  65.5 1.1 copy.42
  66.6 1.0 fusion.11
  67.6 1.2 copy.45
  68.8 0.9 copy.44
  69.7 53.5 %while.24 = (s32[]{:T(128)}, bf16[2,128,768]{1,2,0:T(8,128)(2,1)}, f32[128,6]{0,1:T(8,128)S(1)}, f32[128,6]{0,1:T(8,128)S(1)}, f32[128,6,128]{2,0,1:T(8,128)S(1)...) while((s32[]{:T(128)}, bf16[2,128,768]{1,2,0:T(8,128)(2,1)}, ...), condition=%wide.region_17.18_spmd, body=%wide.region_13.17_spmd.sunk | while | flops 51414596 | bytes 5751247 | solution.py:168
  69.7 2.2 %collective-permute-start = (bf16[2,128,768]{1,2,0:T(8,128)(2,1)}, bf16[2,128,768]{1,2,0:T(8,128)(2,1)S(1)}, u32[]{:S(2)}, u32[]{:S(2)}) collective-permute-start(bf16[2,128,768]{1,2,0:T(8,128)(2,1)} %get-tuple-element.501), channel_id=1, source_target_pairs={{0,1},{1,2},{2,3},{3,4},{4,5},{5,6},{6,7},{7,8},{8,9},{9,10},{10,1... | collective-permute-start | bytes 1179656 | tf_op jit(solution)/shard_map/while/body/eval_jaxpr/ppermute | solution.py:40
  74.5 2.4 %collective-permute-done = bf16[2,128,768]{1,2,0:T(8,128)(2,1)S(1)} collective-permute-done((bf16[2,128,768]{1,2,0:T(8,128)(2,1)}, bf16[2,128,768]{1,2,0:T(8,128)(2,1)S(1)}, u32[]{:S(2)}, u32[]{:S(2)}) %collective-permute-start) | collective-permute-done | bytes 393248 | tf_op jit(solution)/shard_map/while/body/eval_jaxpr/ppermute | solution.py:40
  78.5 2.4 %collective-permute-start = (bf16[2,128,768]{1,2,0:T(8,128)(2,1)}, bf16[2,128,768]{1,2,0:T(8,128)(2,1)S(1)}, u32[]{:S(2)}, u32[]{:S(2)}) collective-permute-start(bf16[2,128,768]{1,2,0:T(8,128)(2,1)} %get-tuple-element.501), channel_id=1, source_target_pairs={{0,1},{1,2},{2,3},{3,4},{4,5},{5,6},{6,7},{7,8},{8,9},{9,10},{10,1... | collective-permute-start | bytes 1179656 | tf_op jit(solution)/shard_map/while/body/eval_jaxpr/ppermute | solution.py:40
  83.4 2.4 %collective-permute-done = bf16[2,128,768]{1,2,0:T(8,128)(2,1)S(1)} collective-permute-done((bf16[2,128,768]{1,2,0:T(8,128)(2,1)}, bf16[2,128,768]{1,2,0:T(8,128)(2,1)S(1)}, u32[]{:S(2)}, u32[]{:S(2)}) %collective-permute-start) | collective-permute-done | bytes 393248 | tf_op jit(solution)/shard_map/while/body/eval_jaxpr/ppermute | solution.py:40
  87.4 2.4 %collective-permute-start = (bf16[2,128,768]{1,2,0:T(8,128)(2,1)}, bf16[2,128,768]{1,2,0:T(8,128)(2,1)S(1)}, u32[]{:S(2)}, u32[]{:S(2)}) collective-permute-start(bf16[2,128,768]{1,2,0:T(8,128)(2,1)} %get-tuple-element.501), channel_id=1, source_target_pairs={{0,1},{1,2},{2,3},{3,4},{4,5},{5,6},{6,7},{7,8},{8,9},{9,10},{10,1... | collective-permute-start | bytes 1179656 | tf_op jit(solution)/shard_map/while/body/eval_jaxpr/ppermute | solution.py:40
  92.4 2.4 %collective-permute-done = bf16[2,128,768]{1,2,0:T(8,128)(2,1)S(1)} collective-permute-done((bf16[2,128,768]{1,2,0:T(8,128)(2,1)}, bf16[2,128,768]{1,2,0:T(8,128)(2,1)S(1)}, u32[]{:S(2)}, u32[]{:S(2)}) %collective-permute-start) | collective-permute-done | bytes 393248 | tf_op jit(solution)/shard_map/while/body/eval_jaxpr/ppermute | solution.py:40
  96.4 2.4 %collective-permute-start = (bf16[2,128,768]{1,2,0:T(8,128)(2,1)}, bf16[2,128,768]{1,2,0:T(8,128)(2,1)S(1)}, u32[]{:S(2)}, u32[]{:S(2)}) collective-permute-start(bf16[2,128,768]{1,2,0:T(8,128)(2,1)} %get-tuple-element.501), channel_id=1, source_target_pairs={{0,1},{1,2},{2,3},{3,4},{4,5},{5,6},{6,7},{7,8},{8,9},{9,10},{10,1... | collective-permute-start | bytes 1179656 | tf_op jit(solution)/shard_map/while/body/eval_jaxpr/ppermute | solution.py:40
  101.3 2.4 %collective-permute-done = bf16[2,128,768]{1,2,0:T(8,128)(2,1)S(1)} collective-permute-done((bf16[2,128,768]{1,2,0:T(8,128)(2,1)}, bf16[2,128,768]{1,2,0:T(8,128)(2,1)S(1)}, u32[]{:S(2)}, u32[]{:S(2)}) %collective-permute-start) | collective-permute-done | bytes 393248 | tf_op jit(solution)/shard_map/while/body/eval_jaxpr/ppermute | solution.py:40
  105.3 2.4 %collective-permute-start = (bf16[2,128,768]{1,2,0:T(8,128)(2,1)}, bf16[2,128,768]{1,2,0:T(8,128)(2,1)S(1)}, u32[]{:S(2)}, u32[]{:S(2)}) collective-permute-start(bf16[2,128,768]{1,2,0:T(8,128)(2,1)} %get-tuple-element.501), channel_id=1, source_target_pairs={{0,1},{1,2},{2,3},{3,4},{4,5},{5,6},{6,7},{7,8},{8,9},{9,10},{10,1... | collective-permute-start | bytes 1179656 | tf_op jit(solution)/shard_map/while/body/eval_jaxpr/ppermute | solution.py:40
  110.3 2.4 %collective-permute-done = bf16[2,128,768]{1,2,0:T(8,128)(2,1)S(1)} collective-permute-done((bf16[2,128,768]{1,2,0:T(8,128)(2,1)}, bf16[2,128,768]{1,2,0:T(8,128)(2,1)S(1)}, u32[]{:S(2)}, u32[]{:S(2)}) %collective-permute-start) | collective-permute-done | bytes 393248 | tf_op jit(solution)/shard_map/while/body/eval_jaxpr/ppermute | solution.py:40
  114.3 2.4 %collective-permute-start = (bf16[2,128,768]{1,2,0:T(8,128)(2,1)}, bf16[2,128,768]{1,2,0:T(8,128)(2,1)S(1)}, u32[]{:S(2)}, u32[]{:S(2)}) collective-permute-start(bf16[2,128,768]{1,2,0:T(8,128)(2,1)} %get-tuple-element.501), channel_id=1, source_target_pairs={{0,1},{1,2},{2,3},{3,4},{4,5},{5,6},{6,7},{7,8},{8,9},{9,10},{10,1... | collective-permute-start | bytes 1179656 | tf_op jit(solution)/shard_map/while/body/eval_jaxpr/ppermute | solution.py:40
  119.2 2.4 %collective-permute-done = bf16[2,128,768]{1,2,0:T(8,128)(2,1)S(1)} collective-permute-done((bf16[2,128,768]{1,2,0:T(8,128)(2,1)}, bf16[2,128,768]{1,2,0:T(8,128)(2,1)S(1)}, u32[]{:S(2)}, u32[]{:S(2)}) %collective-permute-start) | collective-permute-done | bytes 393248 | tf_op jit(solution)/shard_map/while/body/eval_jaxpr/ppermute | solution.py:40
  124.0 1.4 gather_fusion.2
  125.7 3.8 %collective-permute-start.2 = (bf16[1,16,1536]{2,1,0:T(8,128)(2,1)S(1)}, bf16[1,16,1536]{2,1,0:T(8,128)(2,1)S(1)}, u32[]{:S(2)}, u32[]{:S(2)}) collective-permute-start(bf16[1,16,1536]{2,1,0:T(8,128)(2,1)S(1)} %get-tuple-element.375), channel_id=1, source_target_pairs={{0,1},{1,0},{2,3},{3,2},{4,5},{5,4},{6,7},{7,6},{8,9},{9,8},{10,11... | collective-permute-start | bytes 147464 | tf_op jit(solution)/shard_map/ppermute | solution.py:28
  129.6 1.9 %collective-permute-start.4 = (bf16[1,16,1536]{2,1,0:T(8,128)(2,1)S(1)}, bf16[1,16,1536]{2,1,0:T(8,128)(2,1)S(1)}, u32[]{:S(2)}, u32[]{:S(2)}) collective-permute-start(bf16[1,16,1536]{2,1,0:T(8,128)(2,1)S(1)} %get-tuple-element.373), channel_id=1, source_target_pairs={{0,3},{1,2},{2,1},{3,0},{4,7},{5,6},{6,5},{7,4},{8,11},{9,10},{10,... | collective-permute-start | bytes 147464 | tf_op jit(solution)/shard_map/ppermute | solution.py:28
  131.5 11.3 %collective-permute-start.5 = (bf16[1,16,1536]{2,1,0:T(8,128)(2,1)S(1)}, bf16[1,16,1536]{2,1,0:T(8,128)(2,1)S(1)}, u32[]{:S(2)}, u32[]{:S(2)}) collective-permute-start(bf16[1,16,1536]{2,1,0:T(8,128)(2,1)S(1)} %get-tuple-element.372), channel_id=1, source_target_pairs={{0,4},{1,5},{2,6},{3,7},{4,0},{5,1},{6,2},{7,3},{8,12},{9,13},{10,... | collective-permute-start | bytes 147464 | tf_op jit(solution)/shard_map/ppermute | solution.py:28
  142.8 1.5 collective-permute-start.7
  144.3 1.6 collective-permute-start.8
  146.0 2.4 %collective-permute-start.10 = (bf16[1,16,1536]{2,1,0:T(8,128)(2,1)S(1)}, bf16[1,16,1536]{2,1,0:T(8,128)(2,1)S(1)}, u32[]{:S(2)}, u32[]{:S(2)}) collective-permute-start(bf16[1,16,1536]{2,1,0:T(8,128)(2,1)S(1)} %get-tuple-element.367), channel_id=1, source_target_pairs={{0,9},{1,8},{2,11},{3,10},{4,13},{5,12},{6,15},{7,14},{8,1},{9,0},... | collective-permute-start | bytes 147464 | tf_op jit(solution)/shard_map/ppermute | solution.py:28
  149.0 3.3 %collective-permute-start.12 = (bf16[1,16,1536]{2,1,0:T(8,128)(2,1)S(1)}, bf16[1,16,1536]{2,1,0:T(8,128)(2,1)S(1)}, u32[]{:S(2)}, u32[]{:S(2)}) collective-permute-start(bf16[1,16,1536]{2,1,0:T(8,128)(2,1)S(1)} %get-tuple-element.365), channel_id=1, source_target_pairs={{0,11},{1,10},{2,9},{3,8},{4,15},{5,14},{6,13},{7,12},{8,3},{9,2},... | collective-permute-start | bytes 147464 | tf_op jit(solution)/shard_map/ppermute | solution.py:28
  152.7 1.2 collective-permute-start.14
  154.7 2.4 %collective-permute-start.16 = (bf16[1,16,1536]{2,1,0:T(8,128)(2,1)S(1)}, bf16[1,16,1536]{2,1,0:T(8,128)(2,1)S(1)}, u32[]{:S(2)}, u32[]{:S(2)}) collective-permute-start(bf16[1,16,1536]{2,1,0:T(8,128)(2,1)S(1)} %get-tuple-element.361), channel_id=1, source_target_pairs={{0,15},{1,14},{2,13},{3,12},{4,11},{5,10},{6,9},{7,8},{8,7},{9,6},... | collective-permute-start | bytes 147464 | tf_op jit(solution)/shard_map/ppermute | solution.py:28
  157.1 5.0 %collective-permute-done.13 = bf16[1,16,1536]{2,1,0:T(8,128)(2,1)S(1)} collective-permute-done((bf16[1,16,1536]{2,1,0:T(8,128)(2,1)S(1)}, bf16[1,16,1536]{2,1,0:T(8,128)(2,1)S(1)}, u32[]{:S(2)}, u32[]{:S(2)}) %collective-permute-start.13) | collective-permute-done | bytes 49184 | tf_op jit(solution)/shard_map/ppermute | solution.py:28
  162.1 2.2 %collective-permute-done.14 = bf16[1,16,1536]{2,1,0:T(8,128)(2,1)S(1)} collective-permute-done((bf16[1,16,1536]{2,1,0:T(8,128)(2,1)S(1)}, bf16[1,16,1536]{2,1,0:T(8,128)(2,1)S(1)}, u32[]{:S(2)}, u32[]{:S(2)}) %collective-permute-start.14) | collective-permute-done | bytes 49184 | tf_op jit(solution)/shard_map/ppermute | solution.py:28
  164.3 1.5 collective-permute-done.16
  165.8 0.9 gather_fusion.3
  166.8 0.9 broadcast_select_fusion.3
  (172 shorter events, 31.0 us)
Async XLA Ops:
  0.0 123.4 %copy-start = (bf16[768,1536]{1,0:T(8,128)(2,1)S(1)}, bf16[768,1536]{1,0:T(8,128)(2,1)}, u32[]{:S(2)}) copy-start(bf16[768,1536]{1,0:T(8,128)(2,1)} %param.11) | copy-start | bytes 7077892
  10.5 6.7 %copy-start.9 = (s32[2,16]{1,0:T(2,128)S(1)}, s32[2,16]{1,0:T(2,128)}, u32[]{:S(2)}) copy-start(s32[2,16]{1,0:T(2,128)} %param.9) | copy-start | bytes 388
  10.5 34.3 %all-to-all-start = ((bf16[16,16,2304]{2,1,0:T(8,128)(2,1)}), bf16[16,16,2304]{2,1,0:T(8,128)(2,1)S(1)}, u32[]{:S(2)}, u32[]{:S(2)}) async-start(bf16[16,16,2304]{2,1,0:T(8,128)(2,1)} %broadcast_select_fusion), calls=%async_computation | async-start | bytes 2359296 | tf_op jit(solution)/shard_map/all_to_all | solution.py:101
  19.3 4.2 %copy-start.7 = (s32[1,16]{1,0:T(1,128)}, s32[1,16]{1,0:T(1,128)S(1)}, u32[]{:S(2)}) copy-start(s32[1,16]{1,0:T(1,128)S(1)} %get-tuple-element.489) | copy-start | bytes 196
  23.6 1.6 copy-start.12
  48.8 1.8 %copy-start.1 = (bf16[1,128,768]{2,1,0:T(8,128)(2,1)S(1)}, bf16[1,128,768]{2,1,0:T(8,128)(2,1)}, u32[]{:S(2)}) copy-start(bf16[1,128,768]{2,1,0:T(8,128)(2,1)} %get-tuple-element.378) | copy-start | bytes 589828
  48.8 2.6 %copy-start.6 = (s32[256,1]{0,1:T(1,128)S(1)}, s32[256,1]{0,1:T(1,128)}, u32[]{:S(2)}) copy-start(s32[256,1]{0,1:T(1,128)} %get-tuple-element.398) | copy-start | bytes 3076
  48.8 3.8 %copy-start.4 = (s32[1,7]{1,0:T(1,128)S(1)}, s32[1,7]{1,0:T(1,128)}, u32[]{:S(2)}) copy-start(s32[1,7]{1,0:T(1,128)} %param.10) | copy-start | bytes 88
  50.4 3.4 %copy-start.13 = (s32[128]{0:T(128)S(1)}, s32[128]{0:T(128)}, u32[]{:S(2)}) copy-start(s32[128]{0:T(128)} %copy-done.12) | copy-start | bytes 1540
  50.4 4.0 %copy-start.2 = (bf16[128,6,2,1,32]{0,4,3,2,1:T(8,128)(2,1)S(1)}, bf16[128,6,2,1,32]{0,4,3,2,1:T(8,128)(2,1)}, u32[]{:S(2)}) copy-start(bf16[128,6,2,1,32]{0,4,3,2,1:T(8,128)(2,1)} %get-tuple-element.380) | copy-start | bytes 294916
  50.4 4.0 %copy-start.3 = (bf16[128,6,2,1,32]{0,4,3,2,1:T(8,128)(2,1)S(1)}, bf16[128,6,2,1,32]{0,4,3,2,1:T(8,128)(2,1)}, u32[]{:S(2)}) copy-start(bf16[128,6,2,1,32]{0,4,3,2,1:T(8,128)(2,1)} %get-tuple-element.381) | copy-start | bytes 294916
  51.4 11.3 %collective-permute-start.1 = (bf16[2,128,768]{2,1,0:T(8,128)(2,1)}, bf16[2,128,768]{2,1,0:T(8,128)(2,1)S(1)}, u32[]{:S(2)}, u32[]{:S(2)}) collective-permute-start(bf16[2,128,768]{2,1,0:T(8,128)(2,1)} %pad_maximum_fusion), channel_id=1, source_target_pairs={{0,13},{1,14},{2,15},{3,0},{4,1},{5,2},{6,3},{7,4},{8,5},{9,6},{10... | collective-permute-start | bytes 1179656 | tf_op jit(solution)/shard_map/ppermute | solution.py:40
  67.6 2.1 %copy-start.8 = (s32[1,16]{1,0:T(1,128)S(1)}, s32[1,16]{1,0:T(1,128)}, u32[]{:S(2)}) copy-start(s32[1,16]{1,0:T(1,128)} %copy-done.7) | copy-start | bytes 196
  69.7 7.2 %collective-permute-start = (bf16[2,128,768]{1,2,0:T(8,128)(2,1)}, bf16[2,128,768]{1,2,0:T(8,128)(2,1)S(1)}, u32[]{:S(2)}, u32[]{:S(2)}) collective-permute-start(bf16[2,128,768]{1,2,0:T(8,128)(2,1)} %get-tuple-element.501), channel_id=1, source_target_pairs={{0,1},{1,2},{2,3},{3,4},{4,5},{5,6},{6,7},{7,8},{8,9},{9,10},{10,1... | collective-permute-start | bytes 1179656 | tf_op jit(solution)/shard_map/while/body/eval_jaxpr/ppermute | solution.py:40
  78.5 7.4 %collective-permute-start = (bf16[2,128,768]{1,2,0:T(8,128)(2,1)}, bf16[2,128,768]{1,2,0:T(8,128)(2,1)S(1)}, u32[]{:S(2)}, u32[]{:S(2)}) collective-permute-start(bf16[2,128,768]{1,2,0:T(8,128)(2,1)} %get-tuple-element.501), channel_id=1, source_target_pairs={{0,1},{1,2},{2,3},{3,4},{4,5},{5,6},{6,7},{7,8},{8,9},{9,10},{10,1... | collective-permute-start | bytes 1179656 | tf_op jit(solution)/shard_map/while/body/eval_jaxpr/ppermute | solution.py:40
  87.4 7.4 %collective-permute-start = (bf16[2,128,768]{1,2,0:T(8,128)(2,1)}, bf16[2,128,768]{1,2,0:T(8,128)(2,1)S(1)}, u32[]{:S(2)}, u32[]{:S(2)}) collective-permute-start(bf16[2,128,768]{1,2,0:T(8,128)(2,1)} %get-tuple-element.501), channel_id=1, source_target_pairs={{0,1},{1,2},{2,3},{3,4},{4,5},{5,6},{6,7},{7,8},{8,9},{9,10},{10,1... | collective-permute-start | bytes 1179656 | tf_op jit(solution)/shard_map/while/body/eval_jaxpr/ppermute | solution.py:40
  96.4 7.4 %collective-permute-start = (bf16[2,128,768]{1,2,0:T(8,128)(2,1)}, bf16[2,128,768]{1,2,0:T(8,128)(2,1)S(1)}, u32[]{:S(2)}, u32[]{:S(2)}) collective-permute-start(bf16[2,128,768]{1,2,0:T(8,128)(2,1)} %get-tuple-element.501), channel_id=1, source_target_pairs={{0,1},{1,2},{2,3},{3,4},{4,5},{5,6},{6,7},{7,8},{8,9},{9,10},{10,1... | collective-permute-start | bytes 1179656 | tf_op jit(solution)/shard_map/while/body/eval_jaxpr/ppermute | solution.py:40
  105.3 7.4 %collective-permute-start = (bf16[2,128,768]{1,2,0:T(8,128)(2,1)}, bf16[2,128,768]{1,2,0:T(8,128)(2,1)S(1)}, u32[]{:S(2)}, u32[]{:S(2)}) collective-permute-start(bf16[2,128,768]{1,2,0:T(8,128)(2,1)} %get-tuple-element.501), channel_id=1, source_target_pairs={{0,1},{1,2},{2,3},{3,4},{4,5},{5,6},{6,7},{7,8},{8,9},{9,10},{10,1... | collective-permute-start | bytes 1179656 | tf_op jit(solution)/shard_map/while/body/eval_jaxpr/ppermute | solution.py:40
  114.3 7.4 %collective-permute-start = (bf16[2,128,768]{1,2,0:T(8,128)(2,1)}, bf16[2,128,768]{1,2,0:T(8,128)(2,1)S(1)}, u32[]{:S(2)}, u32[]{:S(2)}) collective-permute-start(bf16[2,128,768]{1,2,0:T(8,128)(2,1)} %get-tuple-element.501), channel_id=1, source_target_pairs={{0,1},{1,2},{2,3},{3,4},{4,5},{5,6},{6,7},{7,8},{8,9},{9,10},{10,1... | collective-permute-start | bytes 1179656 | tf_op jit(solution)/shard_map/while/body/eval_jaxpr/ppermute | solution.py:40
  123.9 1.4 copy-start.5
  125.5 4.1 %copy-start.10 = (s32[128]{0:T(128)S(1)}, s32[128]{0:T(128)}, u32[]{:S(2)}) copy-start(s32[128]{0:T(128)} %fusion.31) | copy-start | bytes 1540
  125.7 17.1 %collective-permute-start.2 = (bf16[1,16,1536]{2,1,0:T(8,128)(2,1)S(1)}, bf16[1,16,1536]{2,1,0:T(8,128)(2,1)S(1)}, u32[]{:S(2)}, u32[]{:S(2)}) collective-permute-start(bf16[1,16,1536]{2,1,0:T(8,128)(2,1)S(1)} %get-tuple-element.375), channel_id=1, source_target_pairs={{0,1},{1,0},{2,3},{3,2},{4,5},{5,4},{6,7},{7,6},{8,9},{9,8},{10,11... | collective-permute-start | bytes 147464 | tf_op jit(solution)/shard_map/ppermute | solution.py:28
  129.6 14.7 %collective-permute-start.3 = (bf16[1,16,1536]{2,1,0:T(8,128)(2,1)S(1)}, bf16[1,16,1536]{2,1,0:T(8,128)(2,1)S(1)}, u32[]{:S(2)}, u32[]{:S(2)}) collective-permute-start(bf16[1,16,1536]{2,1,0:T(8,128)(2,1)S(1)} %get-tuple-element.374), channel_id=1, source_target_pairs={{0,2},{1,3},{2,0},{3,1},{4,6},{5,7},{6,4},{7,5},{8,10},{9,11},{10,... | collective-permute-start | bytes 147464 | tf_op jit(solution)/shard_map/ppermute | solution.py:28
  129.6 16.2 %collective-permute-start.4 = (bf16[1,16,1536]{2,1,0:T(8,128)(2,1)S(1)}, bf16[1,16,1536]{2,1,0:T(8,128)(2,1)S(1)}, u32[]{:S(2)}, u32[]{:S(2)}) collective-permute-start(bf16[1,16,1536]{2,1,0:T(8,128)(2,1)S(1)} %get-tuple-element.373), channel_id=1, source_target_pairs={{0,3},{1,2},{2,1},{3,0},{4,7},{5,6},{6,5},{7,4},{8,11},{9,10},{10,... | collective-permute-start | bytes 147464 | tf_op jit(solution)/shard_map/ppermute | solution.py:28
  131.5 14.4 %collective-permute-start.5 = (bf16[1,16,1536]{2,1,0:T(8,128)(2,1)S(1)}, bf16[1,16,1536]{2,1,0:T(8,128)(2,1)S(1)}, u32[]{:S(2)}, u32[]{:S(2)}) collective-permute-start(bf16[1,16,1536]{2,1,0:T(8,128)(2,1)S(1)} %get-tuple-element.372), channel_id=1, source_target_pairs={{0,4},{1,5},{2,6},{3,7},{4,0},{5,1},{6,2},{7,3},{8,12},{9,13},{10,... | collective-permute-start | bytes 147464 | tf_op jit(solution)/shard_map/ppermute | solution.py:28
  142.8 5.5 %collective-permute-start.6 = (bf16[1,16,1536]{2,1,0:T(8,128)(2,1)S(1)}, bf16[1,16,1536]{2,1,0:T(8,128)(2,1)S(1)}, u32[]{:S(2)}, u32[]{:S(2)}) collective-permute-start(bf16[1,16,1536]{2,1,0:T(8,128)(2,1)S(1)} %get-tuple-element.371), channel_id=1, source_target_pairs={{0,5},{1,4},{2,7},{3,6},{4,1},{5,0},{6,3},{7,2},{8,13},{9,12},{10,... | collective-permute-start | bytes 147464 | tf_op jit(solution)/shard_map/ppermute | solution.py:28
  142.8 6.2 %collective-permute-start.7 = (bf16[1,16,1536]{2,1,0:T(8,128)(2,1)S(1)}, bf16[1,16,1536]{2,1,0:T(8,128)(2,1)S(1)}, u32[]{:S(2)}, u32[]{:S(2)}) collective-permute-start(bf16[1,16,1536]{2,1,0:T(8,128)(2,1)S(1)} %get-tuple-element.370), channel_id=1, source_target_pairs={{0,6},{1,7},{2,4},{3,5},{4,2},{5,3},{6,0},{7,1},{8,14},{9,15},{10,... | collective-permute-start | bytes 147464 | tf_op jit(solution)/shard_map/ppermute | solution.py:28
  144.3 8.1 %collective-permute-start.8 = (bf16[1,16,1536]{2,1,0:T(8,128)(2,1)S(1)}, bf16[1,16,1536]{2,1,0:T(8,128)(2,1)S(1)}, u32[]{:S(2)}, u32[]{:S(2)}) collective-permute-start(bf16[1,16,1536]{2,1,0:T(8,128)(2,1)S(1)} %get-tuple-element.369), channel_id=1, source_target_pairs={{0,7},{1,6},{2,5},{3,4},{4,3},{5,2},{6,1},{7,0},{8,15},{9,14},{10,... | collective-permute-start | bytes 147464 | tf_op jit(solution)/shard_map/ppermute | solution.py:28
  145.8 6.9 %collective-permute-start.9 = (bf16[1,16,1536]{2,1,0:T(8,128)(2,1)S(1)}, bf16[1,16,1536]{2,1,0:T(8,128)(2,1)S(1)}, u32[]{:S(2)}, u32[]{:S(2)}) collective-permute-start(bf16[1,16,1536]{2,1,0:T(8,128)(2,1)S(1)} %get-tuple-element.368), channel_id=1, source_target_pairs={{0,8},{1,9},{2,10},{3,11},{4,12},{5,13},{6,14},{7,15},{8,0},{9,1},... | collective-permute-start | bytes 147464 | tf_op jit(solution)/shard_map/ppermute | solution.py:28
  146.0 8.0 %collective-permute-start.10 = (bf16[1,16,1536]{2,1,0:T(8,128)(2,1)S(1)}, bf16[1,16,1536]{2,1,0:T(8,128)(2,1)S(1)}, u32[]{:S(2)}, u32[]{:S(2)}) collective-permute-start(bf16[1,16,1536]{2,1,0:T(8,128)(2,1)S(1)} %get-tuple-element.367), channel_id=1, source_target_pairs={{0,9},{1,8},{2,11},{3,10},{4,13},{5,12},{6,15},{7,14},{8,1},{9,0},... | collective-permute-start | bytes 147464 | tf_op jit(solution)/shard_map/ppermute | solution.py:28
  148.3 6.3 %collective-permute-start.11 = (bf16[1,16,1536]{2,1,0:T(8,128)(2,1)S(1)}, bf16[1,16,1536]{2,1,0:T(8,128)(2,1)S(1)}, u32[]{:S(2)}, u32[]{:S(2)}) collective-permute-start(bf16[1,16,1536]{2,1,0:T(8,128)(2,1)S(1)} %get-tuple-element.366), channel_id=1, source_target_pairs={{0,10},{1,11},{2,8},{3,9},{4,14},{5,15},{6,12},{7,13},{8,2},{9,3},... | collective-permute-start | bytes 147464 | tf_op jit(solution)/shard_map/ppermute | solution.py:28
  149.0 8.0 %collective-permute-start.12 = (bf16[1,16,1536]{2,1,0:T(8,128)(2,1)S(1)}, bf16[1,16,1536]{2,1,0:T(8,128)(2,1)S(1)}, u32[]{:S(2)}, u32[]{:S(2)}) collective-permute-start(bf16[1,16,1536]{2,1,0:T(8,128)(2,1)S(1)} %get-tuple-element.365), channel_id=1, source_target_pairs={{0,11},{1,10},{2,9},{3,8},{4,15},{5,14},{6,13},{7,12},{8,3},{9,2},... | collective-permute-start | bytes 147464 | tf_op jit(solution)/shard_map/ppermute | solution.py:28
  152.4 9.8 %collective-permute-start.13 = (bf16[1,16,1536]{2,1,0:T(8,128)(2,1)S(1)}, bf16[1,16,1536]{2,1,0:T(8,128)(2,1)S(1)}, u32[]{:S(2)}, u32[]{:S(2)}) collective-permute-start(bf16[1,16,1536]{2,1,0:T(8,128)(2,1)S(1)} %get-tuple-element.364), channel_id=1, source_target_pairs={{0,12},{1,13},{2,14},{3,15},{4,8},{5,9},{6,10},{7,11},{8,4},{9,5},... | collective-permute-start | bytes 147464 | tf_op jit(solution)/shard_map/ppermute | solution.py:28
  152.7 11.6 %collective-permute-start.14 = (bf16[1,16,1536]{2,1,0:T(8,128)(2,1)S(1)}, bf16[1,16,1536]{2,1,0:T(8,128)(2,1)S(1)}, u32[]{:S(2)}, u32[]{:S(2)}) collective-permute-start(bf16[1,16,1536]{2,1,0:T(8,128)(2,1)S(1)} %get-tuple-element.363), channel_id=1, source_target_pairs={{0,13},{1,12},{2,15},{3,14},{4,9},{5,8},{6,11},{7,10},{8,5},{9,4},... | collective-permute-start | bytes 147464 | tf_op jit(solution)/shard_map/ppermute | solution.py:28
  153.9 10.4 %collective-permute-start.15 = (bf16[1,16,1536]{2,1,0:T(8,128)(2,1)S(1)}, bf16[1,16,1536]{2,1,0:T(8,128)(2,1)S(1)}, u32[]{:S(2)}, u32[]{:S(2)}) collective-permute-start(bf16[1,16,1536]{2,1,0:T(8,128)(2,1)S(1)} %get-tuple-element.362), channel_id=1, source_target_pairs={{0,14},{1,15},{2,12},{3,13},{4,10},{5,11},{6,8},{7,9},{8,6},{9,7},... | collective-permute-start | bytes 147464 | tf_op jit(solution)/shard_map/ppermute | solution.py:28
  154.7 11.2 %collective-permute-start.16 = (bf16[1,16,1536]{2,1,0:T(8,128)(2,1)S(1)}, bf16[1,16,1536]{2,1,0:T(8,128)(2,1)S(1)}, u32[]{:S(2)}, u32[]{:S(2)}) collective-permute-start(bf16[1,16,1536]{2,1,0:T(8,128)(2,1)S(1)} %get-tuple-element.361), channel_id=1, source_target_pairs={{0,15},{1,14},{2,13},{3,12},{4,11},{5,10},{6,9},{7,8},{8,7},{9,6},... | collective-permute-start | bytes 147464 | tf_op jit(solution)/shard_map/ppermute | solution.py:28
  165.8 0.9 copy-start.11
